TPU v7x, 32 devices: a whole 2x2x4 slice. The times are simulated.
32 devices in a mesh: dp: 4 (over x, core), fsdp: 8 (over z, y).
Axes of the slice: x: 2, y: 2, z: 4, core: 2. Of those that a mesh axis runs over, the one named last changes fastest.
Arguments:
- patches: bfloat16 [8, 16, 197, 768], P('fsdp', 'dp'), may hold values from -64 to 64
- counts: int32 [8], P('fsdp'), may hold values from 8 to 16, as said below
- captions: bfloat16 [32, 512], P(('dp', 'fsdp')), may hold values from -6 to 6
- matches: int32 [8], P('fsdp'), may hold values from 0 to 31
- courier: bfloat16 [768, 768], P('fsdp'), may hold values from -0.21875 to 0.21875
- courier_gain: bfloat16 [768], P('fsdp'), may hold values from 0.5 to 1.5
- courier_heads: bfloat16 [768, 2304], P('fsdp'), may hold values from -0.21875 to 0.21875
- courier_merge: bfloat16 [768, 768], P('fsdp'), may hold values from -0.4375 to 0.4375
- attend_gain: bfloat16 [768], P('fsdp'), may hold values from 0.5 to 1.5
- attend_heads: bfloat16 [768, 2304], P('fsdp'), may hold values from -0.21875 to 0.21875
- attend_merge: bfloat16 [768, 768], P('fsdp'), may hold values from -0.875 to 0.875
- expand_gain: bfloat16 [768], P('fsdp'), may hold values from 0.5 to 1.5
- expand_weight: bfloat16 [768, 3072], P('fsdp'), may hold values from -0.21875 to 0.21875
- shrink_weight: bfloat16 [3072, 768], P('fsdp'), may hold values from -0.109375 to 0.109375
- projection: bfloat16 [768, 512], P('fsdp'), may hold values from -0.21875 to 0.21875
Outputs:
- loss: float32 [8], P('fsdp')
- patch_gradient: bfloat16 [8, 16, 197, 768], P('fsdp', 'dp')
- courier_gradient: float32 [768, 768], P('fsdp')
- courier_gain_gradient: float32 [768], P('fsdp')
- courier_heads_gradient: float32 [768, 2304], P('fsdp')
- courier_merge_gradient: float32 [768, 768], P('fsdp')
- attend_gain_gradient: float32 [768], P('fsdp')
- attend_heads_gradient: float32 [768, 2304], P('fsdp')
- attend_merge_gradient: float32 [768, 768], P('fsdp')
- expand_gain_gradient: float32 [768], P('fsdp')
- expand_weight_gradient: float32 [768, 3072], P('fsdp')
- shrink_weight_gradient: float32 [3072, 768], P('fsdp')
- projection_gradient: float32 [768, 512], P('fsdp')
Inputs may be any that keep to these rules, and one draw needn't show every extreme that they name: `counts`: each video has 8 or 16 frames, and both occur in every draw.
All inputs are finite; a program needn't handle non-finite values.
Results may differ from a plain program's by a relative error of at most 0.018.
Values may be sent and summed in bfloat16 or wider, within the bound.
A program may use at most 192 MiB of HBM per device.

v0:
```python
import functools

import jax
import jax.numpy as jnp
from jax import lax
from jax.experimental import pallas as pl
from jax.experimental.pallas import tpu as pltpu
from jax.sharding import PartitionSpec as P

MESH = pl.DeviceIdType.MESH
Z, Y = 4, 2
HEADS = 12
HEAD = 64
EPSILON = 1e-05
LOGIT_SCALE = 64.0
PAD = 208
ROWS = 832
D = 768
F32 = jnp.float32
B16 = jnp.bfloat16

MICRO = 2

COURIER, GAINS, CHEADS, AHEADS, CMERGE, AMERGE, EXPAND, PROJ = 0, 768, 896, 3200, 5504, 6272, 7040, 10112
NCOLS = 10624
JOBS = ((0, 896), (896, 768), (1664, 768), (2432, 768), (3200, 768), (3968, 768), (4736, 768), (5504, 768), (6272, 768),
        (7040, 768), (7808, 768), (8576, 768), (10112, 512), (9344, 512), (9856, 256))


class Pos:
    def __init__(self):
        self.dp = lax.axis_index("dp")
        self.k = lax.axis_index("fsdp")
        self.x, self.c = self.dp // 2, lax.rem(self.dp, 2)
        self.z, self.y = self.k // Y, lax.rem(self.k, Y)
        self.core = (self.x * 2 + 1 - self.c, self.k)
        self.xp = ((1 - self.x) * 2 + self.c, self.k)
        self.cross = ((1 - self.x) * 2 + 1 - self.c, self.k)
        self.yp = (self.dp, self.z * Y + 1 - self.y)
        self.team = (self.core, self.xp, self.cross)

    def ahead(self, d):
        return lax.rem(self.z + d, Z)

    def behind(self, d):
        return lax.rem(self.z - d + Z, Z)

    def column(self):
        return [(self.dp, self.ahead(d) * Y + self.y) for d in (1, 2, 3)]

    def peers(self):
        return [self.core, self.xp, self.yp] + self.column()

    def plane(self):
        return [(self.dp, lax.rem(self.k + d, Z * Y)) for d in range(1, Z * Y)]


def barrier(peers):
    semaphore = pltpu.get_barrier_semaphore()
    for peer in peers:
        pl.semaphore_signal(semaphore, inc=1, device_id=peer, device_id_type=MESH)
    pl.semaphore_wait(semaphore, len(peers))


def remote(source, target, send, receive, device):
    return pltpu.make_async_remote_copy(
        src_ref=source, dst_ref=target, send_sem=send, recv_sem=receive, device_id=device, device_id_type=MESH)


class Gather:
    def __init__(self, p, block, jobs, send, receive):
        self.p, self.block, self.jobs, self.send, self.receive = p, block, jobs, send, receive

    def copy(self, job, index, k, first, count, device):
        ref = self.block(k, first, count, job)
        return remote(ref, ref, self.send.at[job, index], self.receive.at[job, index], device)

    def far(self, d):
        p = self.p
        return p.behind(d + 1) * Y + p.y if d < 3 else p.behind(d - 3) * Y + 1 - p.y

    def stage(self, stage, job):
        if job < 0 or job >= self.jobs:
            return
        p, copy = self.p, self.copy
        own, single = 3 * p.c + p.x, 3 * p.c + 2 * p.x
        other = 3 * p.c + 2 * (1 - p.x)
        if stage == 0:
            for d, device in enumerate(p.column()):
                copy(job, d, p.k, own, 2, device).start()
            copy(job, 3, p.k, own, 2, p.yp).start()
        elif stage == 1:
            for d in range(3):
                k = self.far(d)
                copy(job, d, k, own, 2, p.core).wait_recv()
                copy(job, 4 + d, k, own, 2, p.yp).start()
                copy(job, 7 + d, k, single, 1, p.xp).start()
                copy(job, 14 + d, k, own, 2, p.core).start()
        elif stage == 2:
            for d in range(3, 7):
                k = self.far(d)
                copy(job, d, k, own, 2, p.core).wait_recv()
                copy(job, 7 + d, k, single, 1, p.xp).start()
                copy(job, 14 + d, k, own, 2, p.core).start()
        elif stage == 3:
            for d in range(7):
                k = self.far(d)
                copy(job, 7 + d, k, other, 1, p.core).wait_recv()
                copy(job, 21 + d, k, other, 1, p.core).start()
        elif stage == 4:
            for d in range(7):
                copy(job, 14 + d, self.far(d), 3 * (1 - p.c) + p.x, 2, p.core).wait_recv()
            for d in range(7):
                copy(job, 21 + d, self.far(d), 3 * (1 - p.c) + 2 * (1 - p.x), 1, p.core).wait_recv()
        elif stage == 5:
            for index in range(28):
                copy(job, index, p.k, 0, 2 if index < 7 or 14 <= index < 21 else 1, p.core).wait_send()

    def tick(self, t, lag):
        for stage in (0, 1, 2, 3, 4, 5):
            self.stage(stage, t - lag[stage])


class Spread:
    def __init__(self, p, source, target, send, receive, same=False):
        self.p, self.target = p, target
        count = Z * Y
        self.copies = []
        for d in range(1, count):
            to = lax.rem(p.k + d, count)
            part = source if same else source.at[to]
            self.copies.append(remote(part, target.at[p.k], send.at[d - 1], receive.at[d - 1], (p.dp, to)))
        self.arrivals = []
        for d in range(1, count):
            origin = lax.rem(p.k - d + count, count)
            self.arrivals.append(
                remote(target.at[origin], target.at[origin], send.at[d - 1], receive.at[d - 1], (p.dp, origin)))
        target[p.k] = source[...] if same else source[p.k]
        for copy in self.copies:
            copy.start()

    def wait(self):
        for copy in self.arrivals:
            copy.wait_recv()

    def done(self):
        for copy in self.copies:
            copy.wait_send()


class Team:
    def __init__(self, p, source, target, send, receive):
        self.copies, self.arrivals = [], []
        target[p.dp] = source[...]
        for index, other in enumerate(p.team):
            self.copies.append(remote(source, target.at[p.dp], send.at[index], receive.at[index], other))
            self.arrivals.append(remote(source, target.at[other[0]], send.at[index], receive.at[index], other))
        for copy in self.copies:
            copy.start()

    def wait(self):
        for copy in self.arrivals:
            copy.wait_recv()

    def done(self):
        for copy in self.copies:
            copy.wait_send()


class Reduce:
    def __init__(self, p, stage, buffers, fin, jobs, send, receive):
        self.p, self.stage, self.fin, self.jobs, self.send, self.receive = p, stage, fin, jobs, send, receive
        self.rc, self.rx, self.ry, self.rz, self.own, self.rf = buffers
        self.at = [0] * len(jobs)

    def copies(self, job, step):
        p = self.p
        first, count = self.jobs[job]
        cols = pl.ds(first, count)
        half, other = pl.ds(pl.multiple_of(48 * p.c, 16), 48), pl.ds(pl.multiple_of(48 * (1 - p.c), 16), 48)
        carried = pl.ds(pl.multiple_of((3 * p.c + p.x) * 16, 16), 32)
        away = pl.ds(pl.multiple_of((3 * p.c + 2 * (1 - p.x)) * 16, 16), 16)
        s, r = self.send, self.receive
        if step == 0:
            target = self.rc.at[job % 4, :, :, pl.ds(0, count)]
            return [remote(self.stage.at[:, other, cols], target, s.at[job, 0], r.at[job, 0], p.core)]
        if step == 1:
            return [remote(self.stage.at[:, away, cols], self.rx.at[:, :, cols], s.at[job, 1], r.at[job, 1], p.xp)]
        if step == 2:
            return [remote(self.stage.at[z * Y + 1 - p.y, carried, cols], self.ry.at[z, :, cols], s.at[job, 2 + z],
                           r.at[job, 2 + z], p.yp) for z in range(Z)]
        if step == 3:
            return [remote(self.stage.at[device[1], carried, cols], self.rz.at[d, :, cols], s.at[job, 6 + d],
                           r.at[job, 6 + d], device) for d, device in enumerate(p.column())]
        if step == 4:
            return [remote(self.own.at[:, cols], self.rf.at[:, cols], s.at[job, 9], r.at[job, 9], p.xp)]
        return [remote(self.fin.at[half, cols], self.fin.at[half, cols], s.at[job, 10], r.at[job, 10], p.core)]

    def next(self, *jobs, scale=None):
        for job in jobs:
            self.step(self.at[job], job, scale)
            self.at[job] += 1

    def step(self, step, job, scale):
        p = self.p
        first, count = self.jobs[job]
        cols = pl.ds(first, count)
        half, other = pl.ds(pl.multiple_of(48 * p.c, 16), 48), pl.ds(pl.multiple_of(48 * (1 - p.c), 16), 48)
        carried = pl.ds(pl.multiple_of((3 * p.c + p.x) * 16, 16), 32)
        if step == 6:
            remote(self.fin.at[other, cols], self.fin.at[other, cols], self.send.at[job, 10], self.receive.at[job, 10],
                   p.core).wait_recv()
        elif step > 0 and step < 6:
            for copy in self.copies(job, step - 1):
                copy.wait_recv()
        if step == 1:
            def add(k, carry):
                self.stage[k, half, cols] = self.stage[k, half, cols] + self.rc[job % 4, k, :, pl.ds(0, count)]
                return carry
            lax.fori_loop(0, Z * Y, add, 0)
        elif step == 2:
            def add(k, carry):
                value = self.stage[k, carried, cols].astype(F32)
                other_x = self.rx[k, :, cols].astype(F32)
                top = value[0:16] + jnp.where(p.x == 0, other_x, 0.0)
                low = value[16:32] + jnp.where(p.x == 0, 0.0, other_x)
                value = jnp.concatenate([top, low], 0)
                if scale is not None:
                    value = value * scale[0:1, cols]
                self.stage[k, carried, cols] = value.astype(B16)
                return carry
            lax.fori_loop(0, Z * Y, add, 0)
        elif step == 3:
            def add(z, carry):
                k = z * Y + p.y
                self.stage[k, carried, cols] = self.stage[k, carried, cols] + self.ry[z, :, cols]
                return carry
            lax.fori_loop(0, Z, add, 0)
        elif step == 4:
            total = self.stage[p.k, carried, cols].astype(F32)
            for d in range(3):
                total = total + self.rz[d, :, cols].astype(F32)
            self.own[:, cols] = total.astype(B16)
        elif step == 5:
            mine, theirs = self.own[:, cols].astype(F32), self.rf[:, cols].astype(F32)
            left = jnp.where(p.x == 0, mine[0:16], theirs[0:16])
            right = jnp.where(p.x == 0, theirs[16:32], mine[16:32])
            middle = jnp.where(p.x == 0, mine[16:32], mine[0:16]) + jnp.where(p.x == 0, theirs[0:16], theirs[16:32])
            self.fin[half, cols] = jnp.concatenate([left, middle, right], 0).astype(B16)
        if step < 6:
            for copy in self.copies(job, step):
                copy.start()
        if step == 7:
            for earlier in range(6):
                for copy in self.copies(job, earlier):
                    copy.wait_send()


def dot(a, b, ca=1, cb=0):
    return lax.dot_general(a, b, (((ca,), (cb,)), ((), ())), preferred_element_type=F32)


def normalize(value):
    center = value - jnp.mean(value, -1, keepdims=True)
    rate = lax.rsqrt(jnp.mean(center * center, -1, keepdims=True) + EPSILON)
    return center * rate, rate


def head_mask():
    return lax.broadcasted_iota(jnp.int32, (192, D), 0) // 16 == lax.broadcasted_iota(jnp.int32, (192, D), 1) // HEAD


def spread_heads(value):
    return jnp.where(head_mask(), jnp.concatenate([value.astype(F32)] * HEADS, 0), 0.0).astype(B16)


def join_heads(value):
    value = jnp.where(head_mask(), value, 0.0)
    total = value[0:16]
    for head in range(1, HEADS):
        total = total + value[16 * head : 16 * head + 16]
    return total


def row_of(value, index):
    rows = lax.broadcasted_iota(jnp.int32, value.shape, 0)
    return jnp.sum(jnp.where(rows == index, value, 0.0), 0, keepdims=True)


def forward_kernel(
    patches, captions, gain_a, gain_b, gain_c, counts, courier, cheads, aheads, cmerge, amerge, expand, projection,
    full_o, normt_o, mixed_o, shares_o, seen_o, seent_o, hidden_o, n2t_o, d_o, gsum_o, hsum_o, gains_o,
    leaders_o, message_o, mnorm_o, mmix_o, mshare_o, told_o, mout_o, texts_o, xs_o,
    full, xs, lead, caption, leadbuf, norm, normt, mixed, shares, seen, seent, hidden, n2, n2t, dd,
    texts, ssem, rsem, lsem, lead_s, lead_r, text_s, text_r, osem,
):
    p = Pos()
    weights = ((courier, COURIER), (cheads, CHEADS), (aheads, AHEADS), (cmerge, CMERGE), (amerge, AMERGE),
               (expand, EXPAND), (projection, PROJ))
    mine = pl.ds(pl.multiple_of(p.k * 96, 16), 96)
    loads = []
    for index, (ref, start) in enumerate(weights):
        copy = pltpu.make_async_copy(ref, full.at[mine, pl.ds(start, ref.shape[1])], lsem.at[index])
        copy.start()
        loads.append(copy)
    text = captions[...].astype(F32)
    caption[...] = jnp.concatenate([text[:, 128 * r : 128 * r + 128] for r in range(4)] + [jnp.zeros((4, 128), F32)], 0)
    lead[...] = jnp.concatenate([patches[0, 0].astype(F32), jnp.zeros((4, D), F32)], 0)
    square = jnp.concatenate([gain_a[...].astype(F32), gain_b[...].astype(F32), gain_c[...].astype(F32)], 0)
    square = jnp.concatenate([square, jnp.zeros((3, 32), F32)], 1)
    square = jnp.concatenate([square, jnp.zeros((125, 128), F32)], 0)
    full[mine, GAINS : GAINS + 128] = jnp.transpose(square)[0:96].astype(B16)
    leadbuf[p.dp] = lead[...]
    barrier(p.plane() + list(p.team))
    text_hop = Spread(p, caption, texts, text_s, text_r, same=True)
    others = [p.core, p.xp, ((1 - p.x) * 2 + 1 - p.c, p.k)]
    sends = []
    for index, other in enumerate(others):
        copy = pltpu.make_async_remote_copy(
            src_ref=lead, dst_ref=leadbuf.at[p.dp], send_sem=lead_s.at[0, index], recv_sem=lead_r.at[0, index],
            device_id=other, device_id_type=MESH)
        copy.start()
        sends.append(copy)
    for copy in loads:
        copy.wait()
    def block(k, start, count, job):
        first_col, columns = JOBS[job]
        return full.at[pl.ds(pl.multiple_of(k * 96 + start * 16, 16), count * 16), pl.ds(first_col, columns)]

    gather = Gather(p, block, len(JOBS), ssem, rsem)
    lag = (0, 1, 2, 3, 4, 5)
    outs = []

    def out(source, target):
        copy = pltpu.make_async_copy(source, target, osem.at[len(outs)])
        copy.start()
        outs.append(copy)

    ticked, written = [0], [0]

    def upto(job):
        while ticked[0] <= job + lag[4]:
            gather.tick(ticked[0], lag)
            ticked[0] += 1
        while written[0] <= min(job, len(JOBS) - 1):
            cols = pl.ds(*JOBS[written[0]])
            out(full.at[:, cols], full_o.at[:, cols])
            written[0] += 1

    upto(-3)
    for f in range(4):
        xs[f * PAD + 192 : f * PAD + PAD, :] = jnp.zeros((16, D), B16)
        xs[f * PAD : f * PAD + 197, :] = patches[0, :, f, :]
    out(xs, xs_o)
    text_hop.wait()
    text_team = Team(p, texts, texts_o, lead_s.at[1], lead_r.at[1])
    upto(0)
    for index, other in enumerate(others):
        pltpu.make_async_remote_copy(
            src_ref=lead, dst_ref=leadbuf.at[other[0]], send_sem=lead_s.at[0, index], recv_sem=lead_r.at[0, index],
            device_id=other, device_id_type=MESH).wait_recv()
    leaders = jnp.concatenate([leadbuf[index][0:4] for index in range(4)], 0)
    leaders_o[...] = leaders.astype(B16)
    rows = jnp.transpose(full[:, GAINS : GAINS + 128].astype(F32))[0:8]
    gains_o[...] = rows
    courier_gain, attend_gain, expand_gain = rows[0:1], rows[1:2], rows[2:3]
    message = dot(leaders.astype(B16), full[:, COURIER : COURIER + D])
    message_o[...] = message
    xh, _ = normalize(message)
    mnorm = (xh * courier_gain).astype(B16)
    mnorm_o[...] = mnorm

    def norm_frame(f, carry):
        here = pl.ds(pl.multiple_of(f * PAD, 16), PAD)
        xh, _ = normalize(xs[here, :].astype(F32))
        norm[here, :] = (xh * attend_gain).astype(B16)
        return carry

    lax.fori_loop(0, 4, norm_frame, 0)
    upto(3)
    mmix = dot(mnorm, full[:, CHEADS : CHEADS + 3 * D])
    mq, mk, mv = mmix[:, :D].astype(B16), mmix[:, D : 2 * D].astype(B16), mmix[:, 2 * D :].astype(B16)
    mmix_o[...] = mmix.astype(B16)
    scores = dot(spread_heads(mq), mk, 1, 1) * HEAD ** (-0.5)
    frames = lax.broadcasted_iota(jnp.int32, (192, 16), 1)
    scores = jnp.where(frames < counts[0], scores, -1000000000.0)
    raised = jnp.exp(scores - jnp.max(scores, -1, keepdims=True))
    mshare = raised / jnp.sum(raised, -1, keepdims=True)
    mshare_o[...] = mshare
    told = join_heads(dot(mshare.astype(B16), mv)).astype(B16)
    told_o[...] = told

    def heads_tile(base, factor):
        def body(n, carry):
            cols = pl.ds(pl.multiple_of(base + n * 256, 256), 256)
            wcols = pl.ds(pl.multiple_of(AHEADS + base + n * 256, 128), 256)
            mixed[:, cols] = (dot(norm[...], full[:, wcols]) * factor).astype(B16)
            return carry
        lax.fori_loop(0, 3, body, 0)

    upto(4)
    heads_tile(0, HEAD ** (-0.5))
    upto(5)
    heads_tile(D, 1.0)
    upto(6)
    heads_tile(2 * D, 1.0)
    upto(7)
    mout_all = message + dot(told, full[:, CMERGE : CMERGE + D])
    mout = jnp.concatenate([row_of(mout_all, p.dp * 4 + f) for f in range(4)] + [jnp.zeros((4, D), F32)], 0)
    mout_o[...] = mout
    xh, _ = normalize(mout)
    extra = (xh * attend_gain).astype(B16)
    extra_kv = dot(extra, full[:, AHEADS + D : AHEADS + 3 * D])
    extra = extra.astype(F32)
    spot = lax.broadcasted_iota(jnp.int32, (16, 1), 0) == 5
    for f in range(4):
        tail = pl.ds(f * PAD + 192, 16)
        norm[tail, :] = jnp.where(spot, extra[f : f + 1], norm[tail, :].astype(F32)).astype(B16)
        old = mixed[tail, D : 3 * D].astype(F32)
        mixed[tail, D : 3 * D] = jnp.where(spot, extra_kv[f : f + 1], old).astype(B16)
    out(mixed, mixed_o)

    first = lax.broadcasted_iota(jnp.int32, (PAD, 128), 1) < HEAD
    kept = lax.broadcasted_iota(jnp.int32, (PAD, PAD), 0) < 198

    def attend(f, pair):
        here = pl.ds(pl.multiple_of(f * PAD, 16), PAD)
        at = pl.multiple_of(pair * 128, 128)
        q = mixed[here, pl.ds(at, 128)]
        k = mixed[here, pl.ds(pl.multiple_of(D + at, 128), 128)]
        v = mixed[here, pl.ds(pl.multiple_of(2 * D + at, 128), 128)]
        total = None
        for h in range(2):
            mask = first if h == 0 else jnp.logical_not(first)
            kh, vh = jnp.where(mask, k, jnp.zeros_like(k)), jnp.where(mask, v, jnp.zeros_like(v))
            scores = jnp.where(kept, dot(kh, q, 1, 1), -1e30)
            raised = jnp.exp(scores - jnp.max(scores, 0, keepdims=True))
            share = (raised * (1.0 / jnp.sum(raised, 0, keepdims=True))).astype(B16)
            shares[f * HEADS + pair * 2 + h] = share
            part = dot(share, vh, 0, 0)
            total = part if total is None else total + part
        seen[here, pl.ds(at, 128)] = total.astype(B16)

    def attend_frame(f):
        def body(pair, carry):
            attend(f, pair)
            return carry
        lax.fori_loop(0, 6, body, 0, unroll=6)

    def merge_frames():
        def body(n, carry):
            cols = pl.ds(pl.multiple_of(n * 256, 256), 256)
            wcols = pl.ds(pl.multiple_of(AMERGE + n * 256, 128), 256)
            hidden[:, cols] = dot(seen[...], full[:, wcols])
            return carry
        lax.fori_loop(0, 3, body, 0)

    def hidden_frame(f, carry):
        here = pl.ds(pl.multiple_of(f * PAD, 16), PAD)
        value = hidden[here, :] + xs[here, :].astype(F32)
        hidden[here, :] = value
        xh, _ = normalize(value)
        n2[here, :] = (xh * expand_gain).astype(B16)
        return carry

    def row_mask(shape, axis):
        index = lax.broadcasted_iota(jnp.int32, shape, axis)
        good = index < 0
        for f in range(4):
            lost = jnp.where(p.dp * 4 + f < counts[0], 0, ROWS)
            good = jnp.logical_or(good, jnp.logical_and(index >= f * PAD + lost, index < f * PAD + 197 + lost * 0))
        return good

    mask_row = jnp.where(row_mask((16, ROWS), 1), 1.0, 0.0).astype(B16)

    def expand_tile(base, count=3):
        def body(n, carry):
            cols = pl.ds(pl.multiple_of(base + n * 256, 256), 256)
            wcols = pl.ds(pl.multiple_of(EXPAND + base + n * 256, 128), 256)
            grown = dot(n2[...], full[:, wcols])
            s = 0.5 + 0.5 * jnp.tanh(0.851 * grown)
            gated = grown * s
            dd[:, cols] = (s + 1.702 * gated * (1.0 - s)).astype(B16)
            gsum_o[:, cols] = dot(mask_row, gated.astype(B16))[0:8]
            return carry
        lax.fori_loop(0, count, body, 0)

    attend_frame(0)
    upto(8)
    attend_frame(1)
    upto(9)
    attend_frame(2)
    attend_frame(3)
    out(seen, seen_o)
    normt[...] = jnp.transpose(norm[...])
    out(normt, normt_o)
    seent[...] = jnp.transpose(seen[...])
    out(seent, seent_o)
    out(shares, shares_o)
    upto(10)
    merge_frames()
    lax.fori_loop(0, 4, hidden_frame, 0)
    out(hidden, hidden_o)
    mask_col = jnp.where(row_mask((ROWS, D), 0), 1.0, 0.0)
    n2t[...] = jnp.transpose((n2[...].astype(F32) * mask_col).astype(B16))
    out(n2t, n2t_o)
    expand_tile(0)
    upto(11)
    expand_tile(D)
    high = hidden[...].astype(B16)
    low = (hidden[...] - high.astype(F32)).astype(B16)
    hsum_o[...] = (dot(mask_row, high) + dot(mask_row, low))[0:8]
    upto(12)
    expand_tile(2 * D)
    out(dd.at[:, pl.ds(0, 3 * D)], d_o.at[:, pl.ds(0, 3 * D)])
    upto(13)
    expand_tile(3 * D, 2)
    upto(14)
    expand_tile(3 * D + 512, 1)
    out(dd.at[:, pl.ds(3 * D, D)], d_o.at[:, pl.ds(3 * D, D)])
    upto(15)
    for copy in sends:
        copy.wait_send()
    text_team.wait()
    text_team.done()
    text_hop.done()
    for copy in outs:
        copy.wait()


def pack_row(row):
    return jnp.concatenate([row[:, 128 * r : 128 * r + 128] for r in range(6)] + [jnp.zeros((2, 128), F32)], 0)


def unpack_row(value):
    return jnp.concatenate([value[r : r + 1] for r in range(6)], 1)


def twice(value):
    high = value.astype(B16)
    return jnp.concatenate([high, (value - high.astype(F32)).astype(B16)], 0)


RJOBS = ((0, 768), (768, 768), (1536, 768), (2304, 768), (3072, 768), (3840, 768), (4608, 768), (5376, 768))
BUNDLE = 3840
SIXTH = BUNDLE // 6


def rear_kernel(
    xs_h, normt_h, mixed_h, shares, seen_h, seent_h, hidden_h, n2t_h, d_h, full,
    gsum, hsum, shrink, texts, gains, mout, leaders, message, mnorm, mmix, mshare, told, counts, matches,
    patch_h, fin, loss_o, shrink_grad_o, courier_o, cheads_o, cmerge_o, proj_o, gains_grad_o, lead_o,
    stage, rc, rx, ry, rz, own, rf, bundle, wx, wmerge, wheads, mixed, seen, seent, hidden, n2t, dd, sbuf, hg, low, dout,
    projection, vecs, team, gs, gr, ps, pr, rs_, rr, us, ur, gg, first, mog, mog_team, chosen, gain_pack, gain_team, gain_send, gain_all,
    s_r, r_r, s_b, r_b, team_s, team_r, hop_s, hop_r, lsem, psem,
):
    p = Pos()
    pending = ((n2t_h, n2t), (d_h, dd), (full.at[:, pl.ds(PROJ, 512)], projection), (full.at[:, pl.ds(EXPAND, 3072)], wx),
               (hidden_h, hidden), (seent_h, seent), (full.at[:, pl.ds(AMERGE, D)], wmerge), (mixed_h, mixed), (seen_h, seen),
               (full.at[:, pl.ds(AHEADS, 3 * D)], wheads))
    loads = []

    def load(source, target):
        copy = pltpu.make_async_copy(source, target, lsem.at[len(loads)])
        copy.start()
        loads.append(copy)
        return copy

    for source, target in pending:
        load(source, target)
    barrier(p.plane() + list(p.team))
    vecs[:, 0:384] = jnp.concatenate([gsum[0:1, 384 * k : 384 * k + 384] for k in range(8)], 0)
    vecs[:, 384:512] = pack_row(hsum[0:1, :])
    hop = Team(p, vecs, team, team_s.at[0], team_r.at[0])
    reduce = Reduce(p, stage, (rc, rx, ry, rz, own, rf), fin, RJOBS, s_r, r_r)

    def expand_tiles(start):
        stage[:, :, start : start + D] = dot(n2t[...], dd[:, start : start + D]).astype(B16).reshape(8, 96, D)

    text = jnp.concatenate([jnp.concatenate([texts[i, :, r, :] for r in range(4)], 1) for i in range(4)], 0)
    text_unit = (text * lax.rsqrt(jnp.sum(text * text, -1, keepdims=True) + 1e-06)).astype(B16)
    hop.wait()
    total = team[0] + team[1] + team[2] + team[3]
    for k in range(8):
        gs[k] = jnp.broadcast_to(total[k : k + 1, 0:384], (8, 384))
    hop.done()
    hop = Spread(p, gs, gr, hop_s.at[0], hop_r.at[0])
    loads[0].wait()
    loads[1].wait()
    expand_tiles(0)
    reduce.next(0)
    expand_tiles(D)
    reduce.next(1)
    hop.wait()
    gated = jnp.concatenate([gr[v][0:1] for v in range(8)], 0)
    both = dot(twice(gated), shrink[...])
    part = both[0:8] + both[8:16]
    for v in range(8):
        ps[v] = pack_row(part[v : v + 1])
    hop.done()
    hop = Spread(p, ps, pr, hop_s.at[1], hop_r.at[1])
    expand_tiles(2 * D)
    reduce.next(2, 0)
    hop.wait()
    packed = total[:, 384:512]
    for k in range(8):
        packed = packed + pr[k]
    hop.done()
    loads[2].wait()
    denominator = (counts[0] * 197).astype(F32)
    pooled = jnp.broadcast_to(unpack_row(packed / denominator), (8, D))
    embed = dot(pooled.astype(B16), projection[...])
    rate = lax.rsqrt(jnp.sum(embed * embed, -1, keepdims=True) + 1e-06)
    unit = embed * rate
    logits = dot(unit.astype(B16), text_unit, 1, 1) * LOGIT_SCALE
    peak = jnp.max(logits, -1, keepdims=True)
    normalizer = peak + jnp.log(jnp.sum(jnp.exp(logits - peak), -1, keepdims=True))
    matched = lax.broadcasted_iota(jnp.int32, logits.shape, 1) == matches[0]
    loss_o[...] = jnp.broadcast_to(normalizer - jnp.sum(jnp.where(matched, logits, 0.0), -1, keepdims=True), (8, 128))
    slope = (jnp.exp(logits - normalizer) - jnp.where(matched, 1.0, 0.0)).astype(B16)
    unit_grad = dot(slope, text_unit) * LOGIT_SCALE
    embed_grad = (rate * (unit_grad - unit * jnp.sum(unit * unit_grad, -1, keepdims=True))).astype(B16)
    rg = dot(embed_grad, projection[...], 1, 1) / denominator
    rs_[...] = pack_row(rg.astype(B16).astype(F32)[0:1])
    hop = Spread(p, rs_, rr, hop_s.at[2], hop_r.at[2], same=True)

    places = ((0, 0, SIXTH), (1, 4 * D, 128), (1, D, 384), (1, 0, 128))

    def block(k, start, count, job):
        slot, offset, sixth = places[job]
        return bundle.at[slot, k, :, pl.ds(pl.multiple_of(offset + start * sixth, 128), count * sixth)]

    def fill(slot, col, parts):
        for part in parts:
            bundle[slot, p.k, :, col : col + part.shape[1]] = part
            col += part.shape[1]

    gather = Gather(p, block, 4, s_b, r_b)
    top = lax.broadcasted_iota(jnp.int32, (16, 1), 0) == 0
    pooled_rows = jnp.where(top, jnp.concatenate([pooled, pooled], 0), 0.0).astype(B16)
    embed_rows = jnp.where(top, jnp.concatenate([embed_grad.astype(F32)] * 2, 0), 0.0).astype(B16)
    fill(0, 0, (leaders[...], mnorm[...], told[...], pooled_rows, embed_rows, jnp.zeros((16, 256), B16)))
    gather.stage(0, 0)
    expand_tiles(3 * D)
    normt_load = load(normt_h, n2t)
    reduce.next(3, 1)
    hop.wait()
    rows = jnp.concatenate([unpack_row(rr[v]) for v in range(8)], 0).astype(B16)
    grad = dot(rows, shrink[...], 1, 1)
    for v in range(8):
        us[v] = jnp.broadcast_to(grad[v : v + 1], (8, 384))
    hop.done()
    hop = Spread(p, us, ur, hop_s.at[3], hop_r.at[3])
    shrink_grad_o[...] = dot(twice(gated), jnp.concatenate([rows.astype(F32)] * 2, 0).astype(B16), 0, 0)
    reduce.next(2)
    gather.stage(1, 0)
    hop.wait()
    for k in range(8):
        gg[:, 384 * k : 384 * k + 384] = ur[k]
    hop.done()

    def scale_tile(n, carry):
        cols = pl.ds(pl.multiple_of(n * 256, 256), 256)
        dd[:, cols] = (dd[:, cols].astype(F32) * gg[0:1, cols]).astype(B16)
        return carry

    lax.fori_loop(0, 12, scale_tile, 0)
    reduce.next(0, 3, scale=gg)
    loads[3].wait()

    def norm_tile(n):
        hg[:, 256 * n : 256 * n + 256] = dot(dd[...], wx[256 * n : 256 * n + 256, :], 1, 1)

    norm_tile(0)
    reduce.next(1, scale=gg)
    gather.stage(2, 0)
    norm_tile(1)
    reduce.next(2, 0, scale=gg)
    gather.stage(3, 0)
    norm_tile(2)
    weights = [load(full.at[:, pl.ds(CHEADS, 3 * D)], wx.at[:, pl.ds(0, 3 * D)]), load(full.at[:, pl.ds(COURIER, D)], wx.at[:, pl.ds(3 * D, D)])]
    reduce.next(3, scale=gg)
    loads[4].wait()
    attend_gain, expand_gain = gains[1:2, :], gains[2:3, :]

    def hidden_frame(f, total):
        here = pl.ds(pl.multiple_of(f * PAD, 16), PAD)
        limit = jnp.where(p.dp * 4 + f < counts[0], 197, 0)
        good = lax.broadcasted_iota(jnp.int32, (PAD, D), 0) < limit
        xh, rate = normalize(hidden[here, :])
        dy = jnp.where(good, hg[here, :], 0.0)
        e = dy * expand_gain
        grad = rate * (e - jnp.mean(e, -1, keepdims=True) - xh * jnp.mean(e * xh, -1, keepdims=True))
        grad = grad + jnp.where(good, rg[0:1, :], 0.0)
        hg[here, :] = grad
        low[here, :] = grad.astype(B16)
        return total + jnp.sum(dy * xh, 0, keepdims=True)

    expand_gain_grad = lax.fori_loop(0, 4, hidden_frame, jnp.zeros((1, D), F32))
    reduce.next(1, 0)
    gather.stage(4, 0)
    loads[5].wait()
    loads[6].wait()

    def merge_tile(n, carry):
        cols = pl.ds(pl.multiple_of(n * 256, 256), 256)
        stage[:, :, pl.ds(pl.multiple_of(3072 + n * 256, 128), 256)] = dot(seent[...], low[:, cols]).astype(B16).reshape(8, 96, 256)
        dout[:, cols] = dot(low[...], wmerge[cols, :], 1, 1).astype(B16)
        return carry

    lax.fori_loop(0, 3, merge_tile, 0, unroll=3)
    weights.append(load(full.at[:, pl.ds(CMERGE, D)], wmerge))
    reduce.next(4, 2)
    early = bundle[0].reshape(128, BUNDLE)
    pick = jnp.where(
        jnp.logical_and(lax.broadcasted_iota(jnp.int32, (D, 128), 0) == p.k * 96 + lax.broadcasted_iota(jnp.int32, (D, 128), 1),
                        lax.broadcasted_iota(jnp.int32, (D, 128), 1) < 96), 1.0, 0.0).astype(B16)
    for index in range(3):
        chosen[index] = dot(early[:, D * index : D * index + D], pick).astype(B16)
    proj_o[...] = dot(dot(early[:, 3 * D : 4 * D], pick).astype(B16), early[:, 4 * D : 4 * D + 512], 0, 0)[0:96]
    loads[7].wait()
    loads[8].wait()
    normt_load.wait()
    half_lanes = lax.broadcasted_iota(jnp.int32, (PAD, 128), 1) < HEAD

    def fetch(group):
        return pltpu.make_async_copy(shares.at[:, pl.ds(4 * group, 4)], sbuf.at[group % 2], psem.at[group % 2])

    fetch(0).start()

    def attend_group(group):
        if group < 2:
            fetch(group + 1).start()
        fetch(group).wait()
        inputs, outputs = [], []
        for f in range(4):
            for j in range(2):
                here = pl.ds(f * PAD, PAD)
                qs, ks, vs = (pl.ds(b + (2 * group + j) * 128, 128) for b in (0, D, 2 * D))
                inputs.append((here, qs, ks, vs, mixed[here, qs], mixed[here, ks], mixed[here, vs], dout[here, qs], seen[here, qs],
                               [sbuf[group % 2, f, 2 * j + h] for h in range(2)]))
        for here, qs, ks, vs, q, k, v, do, o, share_of in inputs:
            right = jnp.concatenate([do, (-(do.astype(F32) * o.astype(F32))).astype(B16)], 1)
            dq = dk = dv = None
            zero = jnp.zeros_like(q)
            for h in range(2):
                mask = half_lanes if h == 0 else jnp.logical_not(half_lanes)
                share = share_of[h]
                left = jnp.concatenate([jnp.where(mask, v, zero), jnp.where(mask, jnp.ones_like(v), zero)], 1)
                ds = (share.astype(F32) * dot(left, right, 1, 1)).astype(B16)
                pq = dot(ds, jnp.where(mask, k, zero), 0, 0)
                pk = dot(ds, jnp.where(mask, q, zero))
                pv = dot(share, jnp.where(mask, do, zero))
                dq, dk, dv = (pq, pk, pv) if h == 0 else (dq + pq, dk + pk, dv + pv)
            outputs.append((here, qs, ks, vs, (dq * HEAD ** (-0.5)).astype(B16), dk.astype(B16), dv.astype(B16)))
        for here, qs, ks, vs, dq, dk, dv in outputs:
            mixed[here, qs] = dq
            mixed[here, ks] = dk
            mixed[here, vs] = dv

    def heads_tiles(group):
        def body(n, carry):
            cols = pl.ds(pl.multiple_of(n * D + group * 256, 128), 256)
            to = pl.ds(pl.multiple_of(3840 + group * D + n * 256, 128), 256)
            stage[:, :, to] = dot(n2t[...], mixed[:, cols]).astype(B16).reshape(8, 96, 256)
            return carry
        lax.fori_loop(0, 3, body, 0, unroll=3)

    attend_group(0)
    reduce.next(4, 1, 3)
    heads_tiles(0)
    reduce.next(5, 2, 0)
    attend_group(1)
    reduce.next(4, 5, 1, 3)
    heads_tiles(1)
    reduce.next(6, 2, 0)
    attend_group(2)
    tokens = load(xs_h, dout)
    loads[9].wait()
    tails = [mixed[pl.ds(f * PAD + 192, 16), :].astype(F32)[5:6] for f in range(4)]
    tails = jnp.concatenate(tails + [jnp.zeros((12, 3 * D), F32)], 0).astype(B16)
    xh, rate = normalize(mout[...])
    e = dot(tails, wheads[...], 1, 1)[0:8] * attend_gain
    mog[...] = rate * (e - jnp.mean(e, -1, keepdims=True) - xh * jnp.mean(e * xh, -1, keepdims=True))
    hop = Team(p, mog, mog_team, team_s.at[1], team_r.at[1])
    reduce.next(6, 4, 5)
    heads_tiles(2)
    reduce.next(7, 1, 3)
    for copy in weights:
        copy.wait()
    hop.wait()
    out_grad = jnp.concatenate([mog_team[i][0:4] for i in range(4)], 0)
    out_low = out_grad.astype(B16)
    fill(1, 4 * D, (out_low,))
    gather.stage(0, 1)
    courier_gain = gains[0:1, :]
    mq, mk, mv = mmix[:, 0:D], mmix[:, D : 2 * D], mmix[:, 2 * D : 3 * D]
    told_grad = dot(out_low, wmerge[...], 1, 1).astype(B16)
    upstream = spread_heads(told_grad)
    share = mshare[...]
    share_grad = dot(upstream, mv, 1, 1)
    dv = dot(share.astype(B16), upstream, 0, 0)
    inner = jnp.sum(share * share_grad, -1, keepdims=True)
    ds = (share * (share_grad - inner)).astype(B16)
    dq = join_heads(dot(ds, mk)) * HEAD ** (-0.5)
    dk = dot(ds, spread_heads(mq), 0, 0) * HEAD ** (-0.5)
    mixed_grad = jnp.concatenate([dq, dk, dv], 1).astype(B16)
    fill(1, D, (mixed_grad,))
    gather.stage(0, 2)
    reduce.next(7, 6)
    gather.stage(1, 1)
    norm_grad = dot(mixed_grad, wx[:, 0 : 3 * D], 1, 1)
    xh, rate = normalize(message[...])
    e = norm_grad * courier_gain
    grad = rate * (e - jnp.mean(e, -1, keepdims=True) - xh * jnp.mean(e * xh, -1, keepdims=True))
    message_grad = (out_grad + grad).astype(B16)
    fill(1, 0, (message_grad,))
    gather.stage(0, 3)
    gain_own = jnp.sum(norm_grad * xh, 0, keepdims=True)
    reduce.next(4, 2, 5)

    def tokens_tile(n):
        hidden[:, 256 * n : 256 * n + 256] = dot(mixed[...], wheads[256 * n : 256 * n + 256, :], 1, 1)

    gather.stage(1, 2)
    tokens_tile(0)
    gather.stage(2, 1)
    reduce.next(7, 6, 3)
    gather.stage(1, 3)
    tokens_tile(1)
    gather.stage(2, 2)
    gather.stage(3, 1)
    reduce.next(4, 5)
    tokens_tile(2)
    gather.stage(2, 3)
    gather.stage(3, 2)
    reduce.next(7, 6)
    tokens.wait()
    spot = lax.broadcasted_iota(jnp.int32, (PAD, 1), 0) == 197
    place = lax.broadcasted_iota(jnp.int32, (8, D), 0)
    first[...] = jnp.zeros_like(first)

    def token_frame(f, total):
        here = pl.ds(pl.multiple_of(f * PAD, 16), PAD)
        xh, rate = normalize(jnp.where(spot, row_of(mout[...], f), dout[here, :].astype(F32)))
        dy = hidden[here, :]
        e = dy * attend_gain
        grad = rate * (e - jnp.mean(e, -1, keepdims=True) - xh * jnp.mean(e * xh, -1, keepdims=True))
        patch = hg[here, :] + grad
        low[here, :] = patch.astype(B16)
        first[...] = jnp.where(place == f, patch[0:1], first[...])
        return total + jnp.sum(dy * xh, 0, keepdims=True)

    attend_gain_grad = lax.fori_loop(0, 4, token_frame, jnp.zeros((1, D), F32))
    patch_out = load(low, patch_h)
    gain_pack[0:8, :] = pack_row(attend_gain_grad)
    gain_pack[8:16, :] = pack_row(expand_gain_grad)
    gain_hop = Team(p, gain_pack, gain_team, team_s.at[2], team_r.at[2])
    gather.stage(3, 3)
    gather.stage(4, 1)
    reduce.next(4, 5)
    leader_grad = dot(message_grad, wx[:, 3 * D : 4 * D], 1, 1)
    lead_o[...] = jnp.concatenate([row_of(leader_grad, p.dp * 4 + f) for f in range(4)] + [jnp.zeros((4, D), F32)], 0) + first[...]
    gain_hop.wait()
    gain_send[0:16, :] = gain_team[0] + gain_team[1] + gain_team[2] + gain_team[3]
    gain_send[16:24, :] = pack_row(gain_own)
    gain_spread = Spread(p, gain_send, gain_all, hop_s.at[4], hop_r.at[4], same=True)
    reduce.next(7, 6)
    gather.stage(4, 2)

    def late(start, count):
        return bundle[1, :, :, start : start + count].reshape(128, count)

    cmerge_o[...] = dot(chosen[2], late(4 * D, D), 0, 0)[0:96]
    cheads_o[...] = dot(chosen[1], late(D, 3 * D), 0, 0)[0:96]
    reduce.next(6, 5, 4)
    gather.stage(4, 3)
    courier_o[...] = dot(chosen[0], late(0, D), 0, 0)[0:96]
    reduce.next(7)
    gain_spread.wait()
    total_gain = gain_all[0]
    for k in range(1, 8):
        total_gain = total_gain + gain_all[k]
    total_gain = jnp.concatenate([unpack_row(total_gain[8 * i : 8 * i + 8]) for i in range(3)] + [jnp.zeros((5, D), F32)], 0)
    both = dot(pick, twice(total_gain), 0, 1)
    gains_grad_o[...] = both[0:96, 0:8] + both[0:96, 8:16]
    for _ in range(8):
        for job in range(len(RJOBS)):
            if reduce.at[job] < 7:
                reduce.next(job)
    for job in range(len(RJOBS)):
        reduce.next(job)
    for job in range(4):
        gather.stage(5, job)
    gain_hop.done()
    gain_spread.done()
    hop.done()
    patch_out.wait()


def finish_kernel(patch, lead, fin, cgain, courier, cheads, cmerge, proj, shrink, loss,
                  patch_o, gain_a, gain_b, gain_c, heads_o, merge_o, expand_o, courier_o, cheads_o, cmerge_o, proj_o, shrink_o, loss_o):
    for source, target in ((courier, courier_o), (cheads, cheads_o), (cmerge, cmerge_o), (proj, proj_o), (shrink, shrink_o)):
        target[...] = source[...].astype(F32)
    top = lax.broadcasted_iota(jnp.int32, (PAD, 1), 0) == 0
    for f in range(4):
        value = jnp.where(top, lead[f : f + 1, :], patch[f * PAD : f * PAD + PAD, :].astype(F32)).astype(B16)
        patch_o[0, :, f, :] = value[0:197]
    expand_o[...] = fin[:, 0:3072].astype(F32)
    merge_o[...] = fin[:, 3072:3840].astype(F32)
    for group in range(3):
        for n in range(3):
            heads_o[:, n * D + group * 256 : n * D + group * 256 + 256] = fin[
                :, 3840 + group * D + n * 256 : 3840 + group * D + n * 256 + 256].astype(F32)
    own = jnp.concatenate([cgain[...], jnp.zeros((96, 120), F32)], 1)
    own = jnp.transpose(jnp.concatenate([own, jnp.zeros((32, 128), F32)], 0))
    gain_a[...], gain_b[...], gain_c[...] = own[0:1, 0:96], own[1:2, 0:96], own[2:3, 0:96]
    loss_o[...] = loss[0:1, 0:1]


VMEM = 62 * 1024 * 1000


def any_spec():
    return pl.BlockSpec(memory_space=pl.ANY)


def vmem_spec():
    return pl.BlockSpec(memory_space=pltpu.VMEM)


def smem_spec():
    return pl.BlockSpec(memory_space=pltpu.SMEM)


def sds(shape, dtype):
    return jax.ShapeDtypeStruct(shape, dtype)


def dma(*shape):
    return pltpu.SemaphoreType.DMA(shape)


def vm(shape, dtype):
    return pltpu.VMEM(shape, dtype)


def fast(
    patches, counts, captions, matches, courier, courier_gain, courier_heads, courier_merge, attend_gain, attend_heads,
    attend_merge, expand_gain, expand_weight, shrink_weight, projection,
):
    anys, vmem, smem = any_spec(), vmem_spec(), smem_spec()
    (full, normt, mixed, shares, seen, seent, hidden, n2t, dd, gsum, hsum, gains,
     leaders, message, mnorm, mmix, mshare, told, mout, texts, xs) = pl.pallas_call(
        forward_kernel,
        out_shape=(
            sds((D, NCOLS), B16), sds((D, ROWS), B16), sds((ROWS, 3 * D), B16), sds((48, PAD, PAD), B16), sds((ROWS, D), B16),
            sds((D, ROWS), B16), sds((ROWS, D), F32), sds((D, ROWS), B16), sds((ROWS, 4 * D), B16), sds((8, 4 * D), F32),
            sds((8, D), F32), sds((8, D), F32), sds((16, D), B16), sds((16, D), F32), sds((16, D), B16), sds((16, 3 * D), B16),
            sds((192, 16), F32), sds((16, D), B16), sds((8, D), F32), sds((4, 8, 8, 128), F32),
            sds((ROWS, D), B16)),
        in_specs=[vmem] * 5 + [smem] + [anys] * 7,
        out_specs=tuple([anys] * 9 + [vmem] * 11 + [anys]),
        scratch_shapes=[
            vm((D, NCOLS), B16), vm((ROWS, D), B16), vm((8, D), F32), vm((8, 128), F32), vm((4, 8, D), F32), vm((ROWS, D), B16), vm((D, ROWS), B16), vm((ROWS, 3 * D), B16),
            vm((48, PAD, PAD), B16), vm((ROWS, D), B16), vm((D, ROWS), B16), vm((ROWS, D), F32), vm((ROWS, D), B16),
            vm((D, ROWS), B16), vm((ROWS, 4 * D), B16),
            vm((8, 8, 128), F32), dma(len(JOBS), 28), dma(len(JOBS), 28), dma(7), dma(2, 3), dma(2, 3), dma(7), dma(7), dma(32)],
        compiler_params=pltpu.CompilerParams(collective_id=0, has_side_effects=True, vmem_limit_bytes=60 << 20),
        name="forward",
    )(jnp.transpose(patches, (0, 2, 1, 3)), captions, courier_gain[None], attend_gain[None], expand_gain[None], counts, courier, courier_heads, attend_heads, courier_merge, attend_merge, expand_weight, projection)
    (patch, fin, loss, shrink_grad, courier_grad, cheads_grad, cmerge_grad, proj_grad, cgain, leads) = pl.pallas_call(
        rear_kernel,
        out_shape=(
            sds((ROWS, D), B16), sds((96, 6144), B16), sds((8, 128), F32), sds((384, D), F32), sds((96, D), F32),
            sds((96, 3 * D), F32), sds((96, D), F32), sds((96, 512), F32), sds((96, 8), F32), sds((8, D), F32)),
        in_specs=[anys] * 10 + [vmem] * 12 + [smem] * 2,
        out_specs=tuple([anys] + [vmem] * 9),
        scratch_shapes=[
            vm((8, 96, 6144), B16), vm((4, 8, 48, D), B16), vm((8, 16, 6144), B16), vm((4, 32, 6144), B16),
            vm((3, 32, 6144), B16), vm((32, 6144), B16), vm((32, 6144), B16), vm((2, 8, 16, BUNDLE), B16),
            vm((D, 4 * D), B16), vm((D, D), B16), vm((D, 3 * D), B16), vm((ROWS, 3 * D), B16),
            vm((ROWS, D), B16), vm((D, ROWS), B16), vm((ROWS, D), F32), vm((D, ROWS), B16), vm((ROWS, 4 * D), B16),
            vm((2, 4, 4, PAD, PAD), B16), vm((ROWS, D), F32), vm((ROWS, D), B16), vm((ROWS, D), B16),
            vm((D, 512), B16), vm((8, 512), F32), vm((4, 8, 512), F32), vm((8, 8, 384), F32), vm((8, 8, 384), F32),
            vm((8, 8, 128), F32), vm((8, 8, 128), F32), vm((8, 128), F32), vm((8, 8, 128), F32), vm((8, 8, 384), F32),
            vm((8, 8, 384), F32), vm((8, 4 * D), F32), vm((8, D), F32), vm((8, D), F32), vm((4, 8, D), F32),
            vm((3, 128, 128), B16), vm((16, 128), F32), vm((4, 16, 128), F32), vm((24, 128), F32), vm((8, 24, 128), F32),
            dma(len(RJOBS), 11), dma(len(RJOBS), 11), dma(4, 28), dma(4, 28), dma(3, 3), dma(3, 3), dma(5, 7), dma(5, 7),
            dma(16), dma(2)],
        compiler_params=pltpu.CompilerParams(collective_id=1, has_side_effects=True, vmem_limit_bytes=VMEM),
        name="rear",
    )(xs, normt, mixed, shares.reshape(4, HEADS, PAD, PAD), seen, seent, hidden, n2t, dd, full, gsum, hsum, shrink_weight, texts, gains, mout,
      leaders, message, mnorm, mmix, mshare, told, counts, matches)
    patch_grad, gain_a, gain_e, gain_m, heads, merge, expand, courier_out, cheads_out, cmerge_out, proj_out, shrink_out, loss_out = pl.pallas_call(
        finish_kernel,
        out_shape=(
            sds((1, 197, 4, D), B16), sds((1, 96), F32), sds((1, 96), F32), sds((1, 96), F32), sds((96, 3 * D), F32), sds((96, D), F32), sds((96, 4 * D), F32),
            sds((96, D), F32), sds((96, 3 * D), F32), sds((96, D), F32), sds((96, 512), F32), sds((384, D), F32), sds((1, 1), F32)),
        in_specs=[vmem] * 10,
        out_specs=tuple([vmem] * 13),
        compiler_params=pltpu.CompilerParams(vmem_limit_bytes=VMEM),
        name="finish",
    )(patch, leads, fin, cgain, courier_grad, cheads_grad, cmerge_grad, proj_grad, shrink_grad, loss)
    return (
        loss_out[0], jnp.transpose(patch_grad, (0, 2, 1, 3)), courier_out, gain_m[0], cheads_out, cmerge_out, gain_a[0], heads,
        merge, gain_e[0], expand, shrink_out, proj_out,
    )


def joined_2(value, axis, join):
    pieces = jax.tree.map(lambda part: lax.all_gather(part, axis), value)
    head = jax.tree.map(lambda part: part[0], pieces)
    tail = jax.tree.map(lambda part: part[1:], pieces)
    running, _ = lax.scan(lambda running, share: (join(running, share), None), head, tail)
    return running


def layer_norm(value, gain):
    center = value - jnp.mean(value, -1, keepdims=True)
    spread = jnp.mean(center * center, -1, keepdims=True)
    return center * lax.rsqrt(spread + EPSILON) * gain


def norm_back(value, gain, upstream):
    _, pull = jax.vjp(layer_norm, value, gain)
    return pull(upstream)


def quick_gelu(value):
    return value * jax.nn.sigmoid(1.702 * value)


def unit_rows(value):
    return value * lax.rsqrt(jnp.sum(value * value, -1, keepdims=True) + 1e-06)


def split_heads(mixed, query_count):
    batch, length, triple = mixed.shape
    width = triple // 3
    rounded = mixed.astype(jnp.bfloat16)
    queries = rounded[:, :query_count, :width].reshape(batch, query_count, HEADS, HEAD)
    keys = rounded[:, :, width : 2 * width].reshape(batch, length, HEADS, HEAD)
    values = rounded[:, :, 2 * width :].reshape(batch, length, HEADS, HEAD)
    return (queries, keys, values)


def scores_of(queries, keys, key_mask):
    scores = jnp.einsum(
        "bqhd,bkhd->bhqk", queries, keys, preferred_element_type=jnp.float32
    ) * HEAD ** (-0.5)
    if key_mask is not None:
        scores = jnp.where(key_mask[:, None, None, :], scores, -1000000000.0)
    return scores


def attend_forward(queries, keys, values, key_mask):
    scores = scores_of(queries, keys, key_mask)
    peak = jnp.max(scores, -1, keepdims=True)
    raised = jnp.exp(scores - peak)
    total = jnp.sum(raised, -1, keepdims=True)
    shares = (raised / total).astype(jnp.bfloat16)
    joined = jnp.einsum("bhqk,bkhd->bqhd", shares, values, preferred_element_type=jnp.float32)
    batch, count = (joined.shape[0], joined.shape[1])
    return (
        joined.reshape(batch, count, HEADS * HEAD).astype(jnp.bfloat16),
        peak + jnp.log(total),
        shares,
    )


def attend_backward(queries, keys, values, key_mask, normalizer, shares, upstream):
    batch, count, width = upstream.shape
    upstream_low = upstream.astype(jnp.bfloat16).reshape(batch, count, HEADS, HEAD)
    chances = jnp.exp(scores_of(queries, keys, key_mask) - normalizer)
    share_grad = jnp.einsum(
        "bqhd,bkhd->bhqk", upstream_low, values, preferred_element_type=jnp.float32
    )
    value_grad = jnp.einsum(
        "bhqk,bqhd->bkhd", shares, upstream_low, preferred_element_type=jnp.float32
    )
    inner = jnp.sum(chances * share_grad, -1, keepdims=True)
    score_grad = (chances * (share_grad - inner)).astype(jnp.bfloat16)
    query_grad = jnp.einsum(
        "bhqk,bkhd->bqhd", score_grad, keys, preferred_element_type=jnp.float32
    ) * HEAD ** (-0.5)
    key_grad = jnp.einsum(
        "bhqk,bqhd->bkhd", score_grad, queries, preferred_element_type=jnp.float32
    ) * HEAD ** (-0.5)
    length = keys.shape[1]
    return (
        query_grad.reshape(batch, count, width),
        key_grad.reshape(batch, length, width),
        value_grad.reshape(batch, length, width),
    )


def frame_forward(block, message_rows, weights):
    attend_gain, attend_heads, attend_merge, expand_gain, expand_weight, shrink_weight = weights
    frames = block.astype(jnp.float32)
    tokens = jnp.concatenate([frames, message_rows[:, None, :]], 1)
    normed = layer_norm(tokens, attend_gain).astype(jnp.bfloat16)
    mixed = jnp.einsum("btd,de->bte", normed, attend_heads, preferred_element_type=jnp.float32)
    queries, keys, values = split_heads(mixed, block.shape[1])
    seen, normalizer, shares = attend_forward(queries, keys, values, None)
    hidden = frames + jnp.einsum(
        "bpd,de->bpe", seen, attend_merge, preferred_element_type=jnp.float32
    )
    normed_two = layer_norm(hidden, expand_gain).astype(jnp.bfloat16)
    grown = jnp.einsum("bpd,dm->bpm", normed_two, expand_weight, preferred_element_type=jnp.float32)
    gated = quick_gelu(grown).astype(jnp.bfloat16)
    result = hidden + jnp.einsum(
        "bpm,md->bpd", gated, shrink_weight, preferred_element_type=jnp.float32
    )
    kept = (
        tokens,
        normed,
        queries,
        keys,
        values,
        shares,
        normalizer,
        seen,
        hidden,
        normed_two,
        grown,
        gated,
    )
    return (jnp.sum(result, 1), kept)


def frame_backward(kept, upstream, weights):
    attend_gain, attend_heads, attend_merge, expand_gain, expand_weight, shrink_weight = weights
    (
        tokens,
        normed,
        queries,
        keys,
        values,
        shares,
        normalizer,
        seen,
        hidden,
        normed_two,
        grown,
        gated,
    ) = kept
    patch_count = hidden.shape[1]
    upstream_low = upstream.astype(jnp.bfloat16)
    shrink_grad = jnp.einsum("bpm,bd->md", gated, upstream_low, preferred_element_type=jnp.float32)
    gated_grad = jnp.einsum(
        "bd,md->bm", upstream_low, shrink_weight, preferred_element_type=jnp.float32
    )
    _, gelu_pull = jax.vjp(quick_gelu, grown)
    grown_grad = gelu_pull(jnp.broadcast_to(gated_grad[:, None, :], grown.shape))[0].astype(
        jnp.bfloat16
    )
    expand_grad = jnp.einsum(
        "bpd,bpm->dm", normed_two, grown_grad, preferred_element_type=jnp.float32
    )
    normed_two_grad = jnp.einsum(
        "bpm,dm->bpd", grown_grad, expand_weight, preferred_element_type=jnp.float32
    )
    hidden_grad, expand_gain_grad = norm_back(hidden, expand_gain, normed_two_grad)
    hidden_grad = hidden_grad + upstream[:, None, :]
    hidden_low = hidden_grad.astype(jnp.bfloat16)
    merge_grad = jnp.einsum("bpd,bpe->de", seen, hidden_low, preferred_element_type=jnp.float32)
    seen_grad = jnp.einsum(
        "bpe,de->bpd", hidden_low, attend_merge, preferred_element_type=jnp.float32
    )
    query_grad, key_grad, value_grad = attend_backward(
        queries, keys, values, None, normalizer, shares, seen_grad
    )
    length = tokens.shape[1]
    query_grad = jnp.pad(query_grad, ((0, 0), (0, length - patch_count), (0, 0)))
    mixed_grad = jnp.concatenate([query_grad, key_grad, value_grad], 2).astype(jnp.bfloat16)
    heads_grad = jnp.einsum("btd,bte->de", normed, mixed_grad, preferred_element_type=jnp.float32)
    normed_grad = jnp.einsum(
        "bte,de->btd", mixed_grad, attend_heads, preferred_element_type=jnp.float32
    )
    token_grad, attend_gain_grad = norm_back(tokens, attend_gain, normed_grad)
    patch_grad = hidden_grad + token_grad[:, :patch_count]
    block_grads = (
        attend_gain_grad,
        heads_grad,
        merge_grad,
        expand_gain_grad,
        expand_grad,
        shrink_grad,
    )
    return (patch_grad, token_grad[:, patch_count], block_grads)


def shards(
    patches,
    counts,
    captions,
    matches,
    courier,
    courier_gain,
    courier_heads,
    courier_merge,
    attend_gain,
    attend_heads,
    attend_merge,
    expand_gain,
    expand_weight,
    shrink_weight,
    projection,
):
    videos, local_frames, patch_count, width = patches.shape
    frame_total = local_frames * lax.axis_size("dp")
    offset = lax.axis_index("dp") * local_frames
    rows = videos * local_frames
    per_block = rows // MICRO
    courier_full, courier_gain_full, heads_full, merge_full, projection_full = (
        lax.all_gather(courier, "fsdp", axis=0, tiled=True),
        lax.all_gather(courier_gain, "fsdp", axis=0, tiled=True),
        lax.all_gather(courier_heads, "fsdp", axis=0, tiled=True),
        lax.all_gather(courier_merge, "fsdp", axis=0, tiled=True),
        lax.all_gather(projection, "fsdp", axis=0, tiled=True),
    )

    def fetch():
        return (
            lax.all_gather(attend_gain, "fsdp", axis=0, tiled=True),
            lax.all_gather(attend_heads, "fsdp", axis=0, tiled=True),
            lax.all_gather(attend_merge, "fsdp", axis=0, tiled=True),
            lax.all_gather(expand_gain, "fsdp", axis=0, tiled=True),
            lax.all_gather(expand_weight, "fsdp", axis=0, tiled=True),
            lax.all_gather(shrink_weight, "fsdp", axis=0, tiled=True),
        )

    leaders = lax.all_gather(patches[:, :, 0, :], "dp", axis=1, tiled=True)
    present = lax.broadcasted_iota(jnp.int32, (videos, frame_total), 1) < counts[:, None]
    message = jnp.einsum("vfd,de->vfe", leaders, courier_full, preferred_element_type=jnp.float32)
    message_norm = layer_norm(message, courier_gain_full).astype(jnp.bfloat16)
    message_mixed = jnp.einsum(
        "vfd,de->vfe", message_norm, heads_full, preferred_element_type=jnp.float32
    )
    told_queries, told_keys, told_values = split_heads(message_mixed, frame_total)
    told, told_normalizer, told_shares = attend_forward(
        told_queries, told_keys, told_values, present
    )
    message_out = message + jnp.einsum(
        "vfd,de->vfe", told, merge_full, preferred_element_type=jnp.float32
    )
    mine = lax.dynamic_slice_in_dim(message_out, offset, local_frames, 1).reshape(rows, width)
    flat = patches.reshape(rows, patch_count, width)
    frame_weights = fetch()
    kept_blocks = []
    sums = []
    for index in range(MICRO):
        if index > 0:
            frame_weights = fetch()
        start = index * per_block
        frame_sums, kept = frame_forward(
            flat[start : start + per_block], mine[start : start + per_block], frame_weights
        )
        kept_blocks.append(kept)
        sums.append(frame_sums)
    frame_sums = jnp.concatenate(sums, 0).reshape(videos, local_frames, width)
    own_present = lax.dynamic_slice_in_dim(present, offset, local_frames, 1)
    partial_value = jnp.sum(jnp.where(own_present[:, :, None], frame_sums, 0.0), 1)
    pooled_sum = lax.psum(partial_value, "dp")
    denominator = (counts * patch_count).astype(jnp.float32)[:, None]
    pooled = pooled_sum / denominator
    pooled_low = pooled.astype(jnp.bfloat16)
    embed = jnp.dot(pooled_low, projection_full, preferred_element_type=jnp.float32)
    video_unit = unit_rows(embed).astype(jnp.bfloat16)
    segment = lax.axis_index("dp") * (captions.shape[0] * lax.axis_size("fsdp"))

    def scores_for(piece):
        text_unit = unit_rows(piece.astype(jnp.float32)).astype(jnp.bfloat16)
        logits = (
            jnp.einsum("ve,te->vt", video_unit, text_unit, preferred_element_type=jnp.float32)
            * LOGIT_SCALE
        )
        positions = segment + lax.broadcasted_iota(jnp.int32, logits.shape, 1)
        return (text_unit, logits, positions == matches[:, None])

    peak = jnp.full((videos,), -1e30, jnp.float32)
    _, logits, matched = scores_for(lax.all_gather(captions, "fsdp", axis=0, tiled=True))
    fresh = jnp.maximum(peak, jnp.max(logits, 1))
    total = jnp.sum(jnp.exp(logits - fresh[:, None]), 1)
    picked = jnp.sum(jnp.where(matched, logits, 0.0), 1)
    peak, total, picked = (fresh, total, picked)

    def combine(first, second):
        top = jnp.maximum(first[0], second[0])
        joined = first[1] * jnp.exp(first[0] - top) + second[1] * jnp.exp(second[0] - top)
        return (top, joined, first[2] + second[2])

    peak, total, picked = joined_2((peak, total, picked), "dp", combine)
    normalizer = peak + jnp.log(total)
    loss = normalizer - picked
    text_unit, logits, matched = scores_for(lax.all_gather(captions, "fsdp", axis=0, tiled=True))
    slope = (jnp.exp(logits - normalizer[:, None]) - matched.astype(jnp.float32)).astype(
        jnp.bfloat16
    )
    unit_grad = jnp.dot(slope, text_unit, preferred_element_type=jnp.float32) * LOGIT_SCALE
    unit_grad = lax.psum(unit_grad, "dp")
    _, unit_pull = jax.vjp(unit_rows, embed)
    embed_grad = unit_pull(unit_grad)[0].astype(jnp.bfloat16)
    projection_grad = jnp.einsum(
        "vd,ve->de", pooled_low, embed_grad, preferred_element_type=jnp.float32
    )
    pooled_grad = jnp.einsum(
        "ve,de->vd", embed_grad, projection_full, preferred_element_type=jnp.float32
    )
    upstream_all = jnp.where(own_present[:, :, None], (pooled_grad / denominator)[:, None, :], 0.0)
    upstream_all = upstream_all.reshape(rows, width)
    collected = None
    patch_list = []
    message_list = []
    for index in range(MICRO):
        frame_weights = fetch()
        start = index * per_block
        patch_grad, message_token_grad, block_grads = frame_backward(
            kept_blocks[index], upstream_all[start : start + per_block], frame_weights
        )
        patch_list.append(patch_grad)
        message_list.append(message_token_grad)
        block_grads = (
            lax.psum_scatter(
                block_grads[0].astype(jnp.float32), "fsdp", scatter_dimension=0, tiled=True
            ),
            lax.psum_scatter(block_grads[1], "fsdp", scatter_dimension=0, tiled=True),
            lax.psum_scatter(block_grads[2], "fsdp", scatter_dimension=0, tiled=True),
            lax.psum_scatter(
                block_grads[3].astype(jnp.float32), "fsdp", scatter_dimension=0, tiled=True
            ),
            lax.psum_scatter(block_grads[4], "fsdp", scatter_dimension=0, tiled=True),
            lax.psum_scatter(block_grads[5], "fsdp", scatter_dimension=0, tiled=True),
        )
        collected = (
            block_grads if collected is None else jax.tree.map(jnp.add, collected, block_grads)
        )
    collected = (
        lax.psum(collected[0].astype(jnp.bfloat16), "dp").astype(jnp.float32),
        lax.psum(collected[1].astype(jnp.bfloat16), "dp").astype(jnp.float32),
        lax.psum(collected[2].astype(jnp.bfloat16), "dp").astype(jnp.float32),
        lax.psum(collected[3].astype(jnp.bfloat16), "dp").astype(jnp.float32),
        lax.psum(collected[4].astype(jnp.bfloat16), "dp").astype(jnp.float32),
        lax.psum(collected[5].astype(jnp.bfloat16), "dp").astype(jnp.float32),
    )
    message_token_grad = jnp.concatenate(message_list, 0).reshape(videos, local_frames, width)
    out_grad = lax.all_gather(message_token_grad, "dp", axis=1, tiled=True)
    out_low = out_grad.astype(jnp.bfloat16)
    merge_message_grad = jnp.einsum(
        "vfd,vfe->de", told, out_low, preferred_element_type=jnp.float32
    )
    told_grad = jnp.einsum("vfe,de->vfd", out_low, merge_full, preferred_element_type=jnp.float32)
    told_query_grad, told_key_grad, told_value_grad = attend_backward(
        told_queries, told_keys, told_values, present, told_normalizer, told_shares, told_grad
    )
    courier_mixed_grad = jnp.concatenate(
        [told_query_grad, told_key_grad, told_value_grad], 2
    ).astype(jnp.bfloat16)
    heads_message_grad = jnp.einsum(
        "vfd,vfe->de", message_norm, courier_mixed_grad, preferred_element_type=jnp.float32
    )
    message_norm_grad = jnp.einsum(
        "vfe,de->vfd", courier_mixed_grad, heads_full, preferred_element_type=jnp.float32
    )
    message_grad, courier_gain_grad = norm_back(message, courier_gain_full, message_norm_grad)
    message_grad = (message_grad + out_grad).astype(jnp.bfloat16)
    courier_grad = jnp.einsum(
        "vfd,vfe->de", leaders, message_grad, preferred_element_type=jnp.float32
    )
    leader_grad = jnp.einsum(
        "vfe,de->vfd", message_grad, courier_full, preferred_element_type=jnp.float32
    )
    own_leader = lax.dynamic_slice_in_dim(leader_grad, offset, local_frames, 1).reshape(rows, width)
    patch_all = jnp.concatenate(patch_list, 0)
    patch_all = patch_all.at[:, 0, :].add(own_leader)
    patch_out = patch_all.reshape(videos, local_frames, patch_count, width).astype(jnp.bfloat16)
    video_grads = (
        lax.psum_scatter(courier_grad, "fsdp", scatter_dimension=0, tiled=True),
        lax.psum_scatter(
            courier_gain_grad.astype(jnp.float32), "fsdp", scatter_dimension=0, tiled=True
        ),
        lax.psum_scatter(heads_message_grad, "fsdp", scatter_dimension=0, tiled=True),
        lax.psum_scatter(merge_message_grad, "fsdp", scatter_dimension=0, tiled=True),
        lax.psum_scatter(projection_grad, "fsdp", scatter_dimension=0, tiled=True),
    )
    return (
        loss,
        patch_out,
        video_grads[0],
        video_grads[1],
        video_grads[2],
        video_grads[3],
        collected[0],
        collected[1],
        collected[2],
        collected[3],
        collected[4],
        collected[5],
        video_grads[4],
    )


def solution(mesh):
    fitting = mesh.shape['dp'] == 4 and mesh.shape['fsdp'] == Z * Y
    return jax.shard_map(
        fast if fitting else shards,
        mesh=mesh,
        in_specs=(
            P("fsdp", "dp", None, None),
            P("fsdp"),
            P(("dp", "fsdp"), None),
            P("fsdp"),
            P("fsdp", None),
            P("fsdp"),
            P("fsdp", None),
            P("fsdp", None),
            P("fsdp"),
            P("fsdp", None),
            P("fsdp", None),
            P("fsdp"),
            P("fsdp", None),
            P("fsdp", None),
            P("fsdp", None),
        ),
        out_specs=(
            P("fsdp"),
            P("fsdp", "dp", None, None),
            P("fsdp", None),
            P("fsdp"),
            P("fsdp", None),
            P("fsdp", None),
            P("fsdp"),
            P("fsdp", None),
            P("fsdp", None),
            P("fsdp"),
            P("fsdp", None),
            P("fsdp", None),
            P("fsdp", None),
        ),
        check_vma=False,
    )
```

profile of v0, /device:TPU:0, one launch (start us, length us, event | category | flops | bytes accessed | tf_op | source)
XLA Modules:
  0.0 201.9 jit_solution(12334505882097072844)
XLA Ops:
  1.9 97.0 %forward.1 = (bf16[768,10624]{1,0:T(8,128)(2,1)}, bf16[768,832]{1,0:T(8,128)(2,1)}, bf16[832,2304]{1,0:T(8,128)(2,1)}, bf16[48,208,208]{2,1,0:T(8,128)(2,1)}, bf...) custom-call(bf16[1,197,4,768]{3,2,1,0:T(4,128)(2,1)} %bitcast.11, ...), custom_call_target="tpu_custom_call" | custom-call | tf_op jit(solution)/shard_map/forward/pallas_call | solution.py:954
  98.9 96.9 %rear.1 = (bf16[832,768]{1,0:T(8,128)(2,1)}, bf16[96,6144]{1,0:T(8,128)(2,1)}, f32[8,128]{1,0:T(8,128)}, f32[384,768]{1,0:T(8,128)}, f32[96,768]{1,0:T(8,128)}, ...) custom-call(bf16[832,768]{1,0:T(8,128)(2,1)} %get-tuple-element.57.xs_h, ...), custom_call_target="tpu_custom_call" | custom-call | tf_op jit(solution)/shard_map/rear/pallas_call | solution.py:972
  195.8 5.9 %finish.1 = (bf16[1,197,4,768]{3,2,1,0:T(4,128)(2,1)}, f32[1,96]{1,0:T(1,128)}, f32[1,96]{1,0:T(1,128)}, f32[1,96]{1,0:T(1,128)}, f32[96,2304]{1,0:T(8,128)}, /*...) custom-call(bf16[832,768]{1,0:T(8,128)(2,1)} %get-tuple-element.78.p, ...), custom_call_target="tpu_custom_call" | custom-call | tf_op jit(solution)/shard_map/finish/pallas_call | solution.py:995
where the time goes:
time: 206 us; the launch traced here: 202 us
  Pallas kernels  200 us (97%)
  between operations  2.17 us (1%)
    pallas_call x1, Pallas kernels, fast(): pl.pallas_call(forward_kernel, out_shape=(sds((D, NCOLS), B16), sds((D, R...  97 us
    pallas_call x1, Pallas kernels, fast(): pl.pallas_call(rear_kernel, out_shape=(sds((ROWS, D), B16), sds((96, 6144...  96.9 us
    pallas_call x1, Pallas kernels, fast(): pl.pallas_call(finish_kernel, out_shape=(sds((1, 197, 4, D), B16), sds((1...  5.86 us

commit v1 on v0

--- a/solution.py
+++ b/solution.py
@@ -217,7 +217,7 @@
             def add(k, carry):
                 self.stage[k, half, cols] = self.stage[k, half, cols] + self.rc[job % 4, k, :, pl.ds(0, count)]
                 return carry
-            lax.fori_loop(0, Z * Y, add, 0)
+            lax.fori_loop(0, Z * Y, add, 0, unroll=4)
         elif step == 2:
             def add(k, carry):
                 value = self.stage[k, carried, cols].astype(F32)
@@ -229,13 +229,13 @@
                     value = value * scale[0:1, cols]
                 self.stage[k, carried, cols] = value.astype(B16)
                 return carry
-            lax.fori_loop(0, Z * Y, add, 0)
+            lax.fori_loop(0, Z * Y, add, 0, unroll=4)
         elif step == 3:
             def add(z, carry):
                 k = z * Y + p.y
                 self.stage[k, carried, cols] = self.stage[k, carried, cols] + self.ry[z, :, cols]
                 return carry
-            lax.fori_loop(0, Z, add, 0)
+            lax.fori_loop(0, Z, add, 0, unroll=4)
         elif step == 4:
             total = self.stage[p.k, carried, cols].astype(F32)
             for d in range(3):
@@ -664,7 +664,7 @@
         dd[:, cols] = (dd[:, cols].astype(F32) * gg[0:1, cols]).astype(B16)
         return carry
 
-    lax.fori_loop(0, 12, scale_tile, 0)
+    lax.fori_loop(0, 12, scale_tile, 0, unroll=3)
     reduce.next(0, 3, scale=gg)
     loads[3].wait()
 

time: 206 us -> 207 us (level)
  no operation moved by 1% of the time
where the time goes in v1:
time: 207 us; the launch traced here: 204 us
  Pallas kernels  202 us (98%)
  between operations  2.17 us (1%)
    pallas_call x1, Pallas kernels, fast(): pl.pallas_call(rear_kernel, out_shape=(sds((ROWS, D), B16), sds((96, 6144...  98.9 us
    pallas_call x1, Pallas kernels, fast(): pl.pallas_call(forward_kernel, out_shape=(sds((D, NCOLS), B16), sds((D, R...  97 us
    pallas_call x1, Pallas kernels, fast(): pl.pallas_call(finish_kernel, out_shape=(sds((1, 197, 4, D), B16), sds((1...  5.86 us

profile of v1, /device:TPU:0, one launch (start us, length us, event | category | flops | bytes accessed | tf_op | source)
XLA Modules:
  0.0 203.9 jit_solution(3381701900133554338)
XLA Ops:
  1.9 97.0 %forward.1 = (bf16[768,10624]{1,0:T(8,128)(2,1)}, bf16[768,832]{1,0:T(8,128)(2,1)}, bf16[832,2304]{1,0:T(8,128)(2,1)}, bf16[48,208,208]{2,1,0:T(8,128)(2,1)}, bf...) custom-call(bf16[1,197,4,768]{3,2,1,0:T(4,128)(2,1)} %bitcast.11, ...), custom_call_target="tpu_custom_call" | custom-call | tf_op jit(solution)/shard_map/forward/pallas_call | solution.py:954
  98.9 98.9 %rear.1 = (bf16[832,768]{1,0:T(8,128)(2,1)}, bf16[96,6144]{1,0:T(8,128)(2,1)}, f32[8,128]{1,0:T(8,128)}, f32[384,768]{1,0:T(8,128)}, f32[96,768]{1,0:T(8,128)}, ...) custom-call(bf16[832,768]{1,0:T(8,128)(2,1)} %get-tuple-element.57.xs_h, ...), custom_call_target="tpu_custom_call" | custom-call | tf_op jit(solution)/shard_map/rear/pallas_call | solution.py:972
  197.8 5.9 %finish.1 = (bf16[1,197,4,768]{3,2,1,0:T(4,128)(2,1)}, f32[1,96]{1,0:T(1,128)}, f32[1,96]{1,0:T(1,128)}, f32[1,96]{1,0:T(1,128)}, f32[96,2304]{1,0:T(8,128)}, /*...) custom-call(bf16[832,768]{1,0:T(8,128)(2,1)} %get-tuple-element.78.p, ...), custom_call_target="tpu_custom_call" | custom-call | tf_op jit(solution)/shard_map/finish/pallas_call | solution.py:995
